TPU v7x, 32 devices: a whole 2x2x4 slice. The times are simulated.
32 devices in a mesh: section: 4 (over y, x), resp: 8 (over z, core).
Axes of the slice: x: 2, y: 2, z: 4, core: 2. Of those that a mesh axis runs over, the one named last changes fastest.
Arguments:
- queries: bfloat16 [4, 512, 4096], P('section', 'resp'), may hold values from -100 to 100
- resp_kv: bfloat16 [4, 512, 1024], P('section', 'resp'), may hold values from -4 to 4
- prefix_kv: bfloat16 [4, 4096, 1024], P('section', 'resp'), may hold values from -6 to 6
- owner: int32 [4, 4], P('section'), may hold values from 0 to 7, as said below
- seg_len: int32 [16, 4], P('resp'), may hold values from 1 to 16, 32 in all within a row
Outputs:
- out: bfloat16 [4, 512, 4096], P('section', 'resp')
Inputs may be any that keep to these rules, and one draw needn't show every extreme that they name: owner[l, p] is one of the devices p * 2 to (p + 1) * 2 - 1, those holding prompt p's responses.
All inputs are finite; a program needn't handle non-finite values.
Results may differ from a plain program's by a relative error of at most 0.0099.
Values may be sent and summed in bfloat16 or wider, within the bound.
A program may use at most 64 MiB of HBM per device.

v0:
```python
import math

import jax
import jax.numpy as jnp
from jax import lax
from jax.sharding import PartitionSpec as P

HQ = 32
HEAD_SIZE = 128
TOKM = 32
MB = 2
PROMPTS = 4


EPS = 1e-06


def swapped(x, axis, stride):
    return lax.ppermute(x, axis, [(i, i ^ 1 << stride) for i in range(lax.axis_size(axis))])


def from_behind(block, axis, distance):
    devices = range(lax.axis_size(axis))
    route = [(i - distance, i) for i in devices if i - distance in devices]
    return lax.ppermute(block, axis, route)


def same_response(lengths, count_of_rows):
    ends = jnp.cumsum(lengths)
    position = jnp.arange(count_of_rows, dtype=jnp.int32)
    response = jnp.sum((position[:, None] >= ends[None, :]).astype(jnp.int32), axis=1)
    return (response[:, None] == response[None, :]) & (position[None, :] <= position[:, None])


def attend(mixed, prefix, local_rows, local_lengths):
    count_of_rows = mixed.shape[0]
    kv_width = prefix.shape[1] // 2
    groups = kv_width // HEAD_SIZE
    heads_of_query = mixed.reshape(count_of_rows, groups, HQ // groups, HEAD_SIZE)
    distant_keys = prefix[:, :kv_width].reshape(-1, groups, HEAD_SIZE)
    distant_values = prefix[:, kv_width:].reshape(-1, groups, HEAD_SIZE)
    nearby_keys = local_rows[:, :kv_width].reshape(-1, groups, HEAD_SIZE)
    nearby_values = local_rows[:, kv_width:].reshape(-1, groups, HEAD_SIZE)
    scaling = 1.0 / math.sqrt(HEAD_SIZE)
    far_scores = (
        jnp.einsum(
            "fiqv,civ->iqfc", heads_of_query, distant_keys, preferred_element_type=jnp.float32
        )
        * scaling
    )
    near_scores = (
        jnp.einsum(
            "fiqv,civ->iqfc", heads_of_query, nearby_keys, preferred_element_type=jnp.float32
        )
        * scaling
    )
    allowed = same_response(local_lengths, count_of_rows)
    near_scores = jnp.where(allowed[None, None], near_scores, -jnp.inf)
    row_top = jnp.maximum(
        jnp.max(far_scores, axis=3, keepdims=True), jnp.max(near_scores, axis=3, keepdims=True)
    )
    far_exp = jnp.exp(far_scores - row_top)
    near_exp = jnp.exp(near_scores - row_top)
    row_total = jnp.sum(far_exp, axis=3, keepdims=True) + jnp.sum(near_exp, axis=3, keepdims=True)
    distant_weights = (far_exp / row_total).astype(jnp.bfloat16)
    nearby_weights = (near_exp / row_total).astype(jnp.bfloat16)
    attended_output = jnp.einsum(
        "euzm,meh->zeuh", distant_weights, distant_values, preferred_element_type=jnp.float32
    )
    attended_output = attended_output + jnp.einsum(
        "euzm,meh->zeuh", nearby_weights, nearby_values, preferred_element_type=jnp.float32
    )
    attended_output = attended_output.reshape(count_of_rows, -1)
    square = jnp.mean(attended_output * attended_output, axis=1, keepdims=True)
    return (attended_output * lax.rsqrt(square + EPS)).astype(jnp.bfloat16)


def local(queries, resp_kv, prefix_kv, owner, seg_len):
    section_index = lax.axis_index("section")
    section_count = lax.axis_size("section")
    devices = lax.axis_size("resp")
    group_size = devices // PROMPTS
    bit_count = group_size.bit_length() - 1
    my_place = lax.axis_index("resp")
    my_rank = my_place % group_size
    my_block = my_place // group_size
    root_rank = (
        jnp.sum(jnp.where(jnp.arange(PROMPTS, dtype=jnp.int32) == my_block, owner[0], 0))
        % group_size
    )
    current = prefix_kv[0]
    for bit_level in range(bit_count):
        incoming = swapped(current, "resp", bit_level)
        holder = (my_rank ^ root_rank) >> bit_level == 0
        current = jnp.where(holder, current, incoming)
    micro_queries = queries[0].reshape(MB, TOKM, -1)
    micro_local = resp_kv[0].reshape(MB, TOKM, -1)
    carried = jnp.zeros((TOKM, micro_queries.shape[2]), jnp.bfloat16)
    results = jnp.zeros_like(micro_queries)
    tick_count = MB + section_count - 1
    for tick_step in range(tick_count):
        micro_index = tick_step - section_index
        is_valid = (micro_index >= 0) & (micro_index < MB)
        clamp_index = jnp.clip(micro_index, 0, MB - 1)
        query_rows = lax.dynamic_index_in_dim(micro_queries, clamp_index, 0, keepdims=False)
        local_rows = lax.dynamic_index_in_dim(micro_local, clamp_index, 0, keepdims=False)
        local_lengths = lax.dynamic_index_in_dim(seg_len, clamp_index, 0, keepdims=False)
        mixed = (query_rows.astype(jnp.float32) + carried.astype(jnp.float32)).astype(jnp.bfloat16)
        normed = attend(mixed, current, local_rows, local_lengths)
        updated = lax.dynamic_update_index_in_dim(results, normed, clamp_index, 0)
        results = jnp.where(is_valid, updated, results)
        if tick_step + 1 < tick_count:
            carried = from_behind(normed, "section", 1)
    return results.reshape(1, MB * TOKM, -1)


def solution(mesh):
    return jax.shard_map(
        local,
        mesh=mesh,
        in_specs=(
            P("section", "resp", None),
            P("section", "resp", None),
            P("section", "resp", None),
            P("section", None),
            P("resp", None),
        ),
        out_specs=P("section", "resp", None),
        check_vma=False,
    )
```

profile of v0, /device:TPU:28, one launch (start us, length us, event | category | flops | bytes accessed | tf_op | source)
XLA Modules:
  0.0 68.0 jit_solution(436506048615795327)
XLA Ops:
  0.0 1.6 %copy.56 = bf16[1,512,1024]{1,2,0:T(8,128)(2,1)S(1)} copy(bf16[1,512,1024]{2,1,0:T(8,128)(2,1)} %param.7) | data formatting | bytes 2097152 | tf_op args[2]
  1.8 0.2 reduce-window.40
  2.2 0.2 reduce-window.41
  2.5 0.2 reduce-window.42
  2.8 0.2 reduce-window.43
  3.1 0.6 fusion.87
  6.0 0.2 reduce-window.44
  6.5 0.5 fusion.104
  7.1 0.1 broadcast_select_fusion
  7.3 0.5 bitcast_reduce_fusion.4
  7.8 0.6 fusion.5
  8.4 0.1 fusion.33
  8.5 0.3 fusion.52
  8.8 1.0 %multiply_reduce_fusion.4 = (f32[32]{0:T(128)S(1)}, f32[32,4,8,128]{3,0,2,1:T(8,128)S(1)}) fusion(f32[4,128,8,32]{1,3,2,0:T(8,128)S(1)} %fusion.52, bf16[512,4,128,1]{0,2,3,1:T(8,128)(2,1)S(1)} %bitcast.253, f32[4,512,32,8]{1,2,3,0:T(8,128)S(1)} %get-tuple-element.28, f32[4,8,32]{2,1,0:T(8,128)S(1)} %add.158, f32[4,8,32]{2,1,0:T(8,128)S(1)} %max.57), kind=kOutput, calls=%fused_computation.84 | convolution fusion | flops 136708064 | bytes 3678336 | tf_op jit(solution)/shard_map/euzm,meh->zeuh/dot_general | solution.py:67
  9.8 0.3 copy.64
  10.1 0.1 reshape.669
  10.2 0.3 fusion.28
  10.5 3.4 %collective-permute-start.1 = (bf16[32,4096]{1,0:T(8,128)(2,1)S(1)}, bf16[32,4096]{1,0:T(8,128)(2,1)S(1)}, u32[]{:S(2)}, u32[]{:S(2)}) collective-permute-start(bf16[32,4096]{1,0:T(8,128)(2,1)S(1)} %fusion.28), channel_id=1, source_target_pairs={{0,8},{8,16},{16,24},{1,9},{9,17},{17,25},{2,10},{10,18},{18,26},{... | collective-permute-start | bytes 786440 | tf_op jit(solution)/shard_map/ppermute | solution.py:25
  14.0 0.1 fusion.39
  14.1 7.9 %collective-permute-done.1 = bf16[32,4096]{1,0:T(8,128)(2,1)S(1)} collective-permute-done((bf16[32,4096]{1,0:T(8,128)(2,1)S(1)}, bf16[32,4096]{1,0:T(8,128)(2,1)S(1)}, u32[]{:S(2)}, u32[]{:S(2)}) %collective-permute-start.1) | collective-permute-done | bytes 262176 | tf_op jit(solution)/shard_map/ppermute | solution.py:25
  22.1 0.5 bitcast_reduce_fusion.3
  22.6 0.5 fusion.105
  23.2 0.6 fusion.6
  23.8 0.1 fusion.34
  23.9 0.3 fusion.53
  24.2 1.0 %multiply_reduce_fusion.3 = (f32[32]{0:T(128)S(1)}, f32[32,4,8,128]{3,0,2,1:T(8,128)S(1)}) fusion(f32[4,128,8,32]{1,3,2,0:T(8,128)S(1)} %fusion.53, bf16[512,4,128,1]{0,2,3,1:T(8,128)(2,1)S(1)} %bitcast.254, f32[4,512,32,8]{1,2,3,0:T(8,128)S(1)} %get-tuple-element.34, f32[4,8,32]{2,1,0:T(8,128)S(1)} %add.163, f32[4,8,32]{2,1,0:T(8,128)S(1)} %max.59), kind=kOutput, calls=%fused_computation.80 | convolution fusion | flops 136708064 | bytes 3678336 | tf_op jit(solution)/shard_map/euzm,meh->zeuh/dot_general | solution.py:67
  25.2 0.3 copy.73
  25.5 0.1 reshape.676
  25.6 0.3 fusion.27
  26.0 2.5 %collective-permute-start.2 = (bf16[32,4096]{1,0:T(8,128)(2,1)S(1)}, bf16[32,4096]{1,0:T(8,128)(2,1)S(1)}, u32[]{:S(2)}, u32[]{:S(2)}) collective-permute-start(bf16[32,4096]{1,0:T(8,128)(2,1)S(1)} %fusion.27), channel_id=1, source_target_pairs={{0,8},{8,16},{16,24},{1,9},{9,17},{17,25},{2,10},{10,18},{18,26},{... | collective-permute-start | bytes 786440 | tf_op jit(solution)/shard_map/ppermute | solution.py:25
  28.4 0.1 fusion.41
  28.6 8.0 %collective-permute-done.2 = bf16[32,4096]{1,0:T(8,128)(2,1)S(1)} collective-permute-done((bf16[32,4096]{1,0:T(8,128)(2,1)S(1)}, bf16[32,4096]{1,0:T(8,128)(2,1)S(1)}, u32[]{:S(2)}, u32[]{:S(2)}) %collective-permute-start.2) | collective-permute-done | bytes 262176 | tf_op jit(solution)/shard_map/ppermute | solution.py:25
  36.8 0.5 bitcast_reduce_fusion.2
  37.3 0.5 fusion.106
  37.8 0.6 fusion.7
  38.4 0.1 fusion.35
  38.6 0.3 fusion.54
  38.9 1.0 %multiply_reduce_fusion.2 = (f32[32]{0:T(128)S(1)}, f32[32,4,8,128]{3,0,2,1:T(8,128)S(1)}) fusion(f32[4,128,8,32]{1,3,2,0:T(8,128)S(1)} %fusion.54, bf16[512,4,128,1]{0,2,3,1:T(8,128)(2,1)S(1)} %bitcast.255, f32[4,512,32,8]{1,2,3,0:T(8,128)S(1)} %get-tuple-element.40, f32[4,8,32]{2,1,0:T(8,128)S(1)} %add.168, f32[4,8,32]{2,1,0:T(8,128)S(1)} %max.61), kind=kOutput, calls=%fused_computation.76 | convolution fusion | flops 136708064 | bytes 3678336 | tf_op jit(solution)/shard_map/euzm,meh->zeuh/dot_general | solution.py:67
  39.9 0.3 copy.82
  40.2 0.1 reshape.683
  40.3 0.3 fusion.26
  40.6 2.1 %collective-permute-start.3 = (bf16[32,4096]{1,0:T(8,128)(2,1)S(1)}, bf16[32,4096]{1,0:T(8,128)(2,1)S(1)}, u32[]{:S(2)}, u32[]{:S(2)}) collective-permute-start(bf16[32,4096]{1,0:T(8,128)(2,1)S(1)} %fusion.26), channel_id=1, source_target_pairs={{0,8},{8,16},{16,24},{1,9},{9,17},{17,25},{2,10},{10,18},{18,26},{... | collective-permute-start | bytes 786440 | tf_op jit(solution)/shard_map/ppermute | solution.py:25
  42.7 0.1 fusion.43
  42.8 7.5 %collective-permute-done.3 = bf16[32,4096]{1,0:T(8,128)(2,1)S(1)} collective-permute-done((bf16[32,4096]{1,0:T(8,128)(2,1)S(1)}, bf16[32,4096]{1,0:T(8,128)(2,1)S(1)}, u32[]{:S(2)}, u32[]{:S(2)}) %collective-permute-start.3) | collective-permute-done | bytes 262176 | tf_op jit(solution)/shard_map/ppermute | solution.py:25
  50.5 0.5 bitcast_reduce_fusion.1
  51.0 0.5 fusion.107
  51.6 0.6 fusion.8
  52.2 0.1 fusion.36
  52.3 0.3 fusion.55
  52.6 1.0 %multiply_reduce_fusion.1 = (f32[32]{0:T(128)S(1)}, f32[32,4,8,128]{3,0,2,1:T(8,128)S(1)}) fusion(f32[4,128,8,32]{1,3,2,0:T(8,128)S(1)} %fusion.55, bf16[512,4,128,1]{0,2,3,1:T(8,128)(2,1)S(1)} %bitcast.256, f32[4,512,32,8]{1,2,3,0:T(8,128)S(1)} %get-tuple-element.46, f32[4,8,32]{2,1,0:T(8,128)S(1)} %add.173, f32[4,8,32]{2,1,0:T(8,128)S(1)} %max.63), kind=kOutput, calls=%fused_computation.72 | convolution fusion | flops 136708064 | bytes 3678336 | tf_op jit(solution)/shard_map/euzm,meh->zeuh/dot_general | solution.py:67
  53.6 0.3 copy.91
  54.0 0.3 fusion.25
  54.3 1.9 %collective-permute-start.4 = (bf16[32,4096]{1,0:T(8,128)(2,1)S(1)}, bf16[32,4096]{1,0:T(8,128)(2,1)S(1)}, u32[]{:S(2)}, u32[]{:S(2)}) collective-permute-start(bf16[32,4096]{1,0:T(8,128)(2,1)S(1)} %fusion.25), channel_id=1, source_target_pairs={{0,8},{8,16},{16,24},{1,9},{9,17},{17,25},{2,10},{10,18},{18,26},{... | collective-permute-start | bytes 786440 | tf_op jit(solution)/shard_map/ppermute | solution.py:25
  56.3 0.1 fusion.45
  56.4 7.1 %collective-permute-done.4 = bf16[32,4096]{1,0:T(8,128)(2,1)S(1)} collective-permute-done((bf16[32,4096]{1,0:T(8,128)(2,1)S(1)}, bf16[32,4096]{1,0:T(8,128)(2,1)S(1)}, u32[]{:S(2)}, u32[]{:S(2)}) %collective-permute-start.4) | collective-permute-done | bytes 262176 | tf_op jit(solution)/shard_map/ppermute | solution.py:25
  63.6 0.5 bitcast_reduce_fusion
  64.1 0.5 fusion.108
  64.7 0.6 fusion.9
  65.3 0.1 fusion.37
  65.4 0.3 fusion.56
  65.7 1.0 %multiply_reduce_fusion = (f32[32]{0:T(128)S(1)}, f32[32,4,8,128]{3,0,2,1:T(8,128)S(1)}) fusion(f32[4,128,8,32]{1,3,2,0:T(8,128)S(1)} %fusion.56, bf16[512,4,128,1]{0,2,3,1:T(8,128)(2,1)S(1)} %bitcast.257, f32[4,512,32,8]{1,2,3,0:T(8,128)S(1)} %get-tuple-element.52, f32[4,8,32]{2,1,0:T(8,128)S(1)} %add.178, f32[4,8,32]{2,1,0:T(8,128)S(1)} %max.65), kind=kOutput, calls=%fused_computation.68 | convolution fusion | flops 136708064 | bytes 3678336 | tf_op jit(solution)/shard_map/euzm,meh->zeuh/dot_general | solution.py:67
  66.7 0.3 copy.100
  67.1 0.1 fusion.47
  67.3 0.8 %copy-done = bf16[2,32,4096]{2,1,0:T(8,128)(2,1)} copy-done((bf16[2,32,4096]{2,1,0:T(8,128)(2,1)}, bf16[2,32,4096]{2,1,0:T(8,128)(2,1)S(1)}, u32[]{:S(2)}) %copy-start) | copy-done | bytes 524312
  (65 shorter events, 2.1 us)
Async XLA Ops:
  0.0 1.7 %copy-start.1 = (bf16[1,64,4096]{2,1,0:T(8,128)(2,1)S(1)}, bf16[1,64,4096]{2,1,0:T(8,128)(2,1)}, u32[]{:S(2)}) copy-start(bf16[1,64,4096]{2,1,0:T(8,128)(2,1)} %param.5) | copy-start | bytes 1572868
  0.0 1.7 %copy-start.2 = (bf16[1,64,1024]{2,1,0:T(8,128)(2,1)S(1)}, bf16[1,64,1024]{2,1,0:T(8,128)(2,1)}, u32[]{:S(2)}) copy-start(bf16[1,64,1024]{2,1,0:T(8,128)(2,1)} %param.6) | copy-start | bytes 393220
  0.0 1.8 %copy-start.3 = (s32[2,4]{1,0:T(2,128)S(1)}, s32[2,4]{1,0:T(2,128)}, u32[]{:S(2)}) copy-start(s32[2,4]{1,0:T(2,128)} %param.9) | copy-start | bytes 100
  0.0 3.1 %copy-start.4 = (s32[1,4]{1,0:T(1,128)S(1)}, s32[1,4]{1,0:T(1,128)}, u32[]{:S(2)}) copy-start(s32[1,4]{1,0:T(1,128)} %param.8) | copy-start | bytes 52
  1.6 5.5 %collective-permute-start = (bf16[512,1024]{0,1:T(8,128)(2,1)S(1)}, bf16[512,1024]{0,1:T(8,128)(2,1)S(1)}, u32[]{:S(2)}, u32[]{:S(2)}) collective-permute-start(bf16[512,1024]{0,1:T(8,128)(2,1)S(1)} %bitcast.236), channel_id=1, source_target_pairs={{0,1},{1,0},{2,3},{3,2},{4,5},{5,4},{6,7},{7,6},{8,9},{9,8},{10,11... | collective-permute-start | bytes 3145736 | tf_op jit(solution)/shard_map/ppermute | solution.py:19
  10.5 11.5 %collective-permute-start.1 = (bf16[32,4096]{1,0:T(8,128)(2,1)S(1)}, bf16[32,4096]{1,0:T(8,128)(2,1)S(1)}, u32[]{:S(2)}, u32[]{:S(2)}) collective-permute-start(bf16[32,4096]{1,0:T(8,128)(2,1)S(1)} %fusion.28), channel_id=1, source_target_pairs={{0,8},{8,16},{16,24},{1,9},{9,17},{17,25},{2,10},{10,18},{18,26},{... | collective-permute-start | bytes 786440 | tf_op jit(solution)/shard_map/ppermute | solution.py:25
  26.0 10.7 %collective-permute-start.2 = (bf16[32,4096]{1,0:T(8,128)(2,1)S(1)}, bf16[32,4096]{1,0:T(8,128)(2,1)S(1)}, u32[]{:S(2)}, u32[]{:S(2)}) collective-permute-start(bf16[32,4096]{1,0:T(8,128)(2,1)S(1)} %fusion.27), channel_id=1, source_target_pairs={{0,8},{8,16},{16,24},{1,9},{9,17},{17,25},{2,10},{10,18},{18,26},{... | collective-permute-start | bytes 786440 | tf_op jit(solution)/shard_map/ppermute | solution.py:25
  40.6 9.8 %collective-permute-start.3 = (bf16[32,4096]{1,0:T(8,128)(2,1)S(1)}, bf16[32,4096]{1,0:T(8,128)(2,1)S(1)}, u32[]{:S(2)}, u32[]{:S(2)}) collective-permute-start(bf16[32,4096]{1,0:T(8,128)(2,1)S(1)} %fusion.26), channel_id=1, source_target_pairs={{0,8},{8,16},{16,24},{1,9},{9,17},{17,25},{2,10},{10,18},{18,26},{... | collective-permute-start | bytes 786440 | tf_op jit(solution)/shard_map/ppermute | solution.py:25
  54.3 9.2 %collective-permute-start.4 = (bf16[32,4096]{1,0:T(8,128)(2,1)S(1)}, bf16[32,4096]{1,0:T(8,128)(2,1)S(1)}, u32[]{:S(2)}, u32[]{:S(2)}) collective-permute-start(bf16[32,4096]{1,0:T(8,128)(2,1)S(1)} %fusion.25), channel_id=1, source_target_pairs={{0,8},{8,16},{16,24},{1,9},{9,17},{17,25},{2,10},{10,18},{18,26},{... | collective-permute-start | bytes 786440 | tf_op jit(solution)/shard_map/ppermute | solution.py:25
  67.2 0.8 %copy-start = (bf16[2,32,4096]{2,1,0:T(8,128)(2,1)}, bf16[2,32,4096]{2,1,0:T(8,128)(2,1)S(1)}, u32[]{:S(2)}) copy-start(bf16[2,32,4096]{2,1,0:T(8,128)(2,1)S(1)} %fusion.47) | copy-start | bytes 1572868
where the time goes:
time: 68.3 us; the launch traced here: 68 us
  waiting for transfers between devices  30.5 us (45%)
  matrix products  11.5 us (17%)
  starting transfers between devices  9.99 us (15%)
  other arithmetic  8.3 us (12%)
  local copies, waits for them, and re-layouts  4.98 us (7%)
  between operations  2.68 us (4%)
    ppermute x4, waiting for transfers between devices, from_behind(): return lax.ppermute(block, axis, route)  30.5 us
    ppermute x4, starting transfers between devices, from_behind(): return lax.ppermute(block, axis, route)  9.92 us
    dot_general x5, matrix products, attend(): jnp.einsum('euzm,meh->zeuh', distant_weights, distant_values, preferred_e...  4.84 us
    reduce_sum x5, other arithmetic, attend(): jnp.sum(far_exp, axis=3, keepdims=True)  2.97 us
    dot_general x5, matrix products, attend(): jnp.einsum('fiqv,civ->iqfc', heads_of_query, nearby_keys, preferred_eleme...  2.74 us
    unnamed x17, local copies, waits for them, and re-layouts  2.6 us
    dot_general x5, matrix products, attend(): jnp.einsum('fiqv,civ->iqfc', heads_of_query, distant_keys, preferred_elem...  2.5 us
    add x5, local copies, waits for them, and re-layouts, attend(): attended_output + jnp.einsum('euzm,meh->zeuh', nearby_weights, nearby_val...  1.54 us
  transfers between devices with their start and end apart: 5, of which 4 were waited for; matrix products, arithmetic and copies ran while one was open for 5% of the time, Pallas kernels for 0%

commit v1 on v0

v1 whole, which is shorter than its diff:
```python
import functools
import math

import jax
import jax.numpy as jnp
from jax import lax
from jax.experimental import pallas as pl
from jax.experimental.pallas import tpu as pltpu
from jax.sharding import PartitionSpec as P

HEAD = 128
GROUP_HEADS = 8
TOKM = 32
MB = 2
RESPS = 4
PROMPTS = 4
CHUNK = 8
EPS = 1e-06
MESH = pl.DeviceIdType.MESH
F32 = jnp.float32
BF16 = jnp.bfloat16


def kernel(
    sections,
    bits,
    q_hbm,
    r_hbm,
    p_hbm,
    owner,
    seg,
    out_hbm,
    q_v,
    r_v,
    p_v,
    vt_own,
    k_in,
    v_in,
    k_all,
    v_all,
    q_t,
    carry,
    sent,
    rows16,
    out_v,
    load_sem,
    out_sem,
    x_send,
    x_recv,
    c_send,
    c_recv,
):
    sec = lax.axis_index("section")
    place = lax.axis_index("resp")
    group = 1 << bits
    rank = lax.rem(place, group)
    block = lax.div(place, group)
    plen = p_v.shape[0]
    kvw = p_v.shape[1] // 2
    pairs = kvw // (2 * HEAD)
    near = r_v.shape[0]
    wide = pairs * 2 * GROUP_HEADS * HEAD
    chunks = near // CHUNK

    load_p = pltpu.make_async_copy(p_hbm.at[0], p_v, load_sem.at[0])
    load_q = pltpu.make_async_copy(q_hbm.at[0], q_v, load_sem.at[1])
    load_r = pltpu.make_async_copy(r_hbm.at[0], r_v, load_sem.at[2])
    load_p.start()
    load_q.start()
    load_r.start()

    partners = []
    for b in range(bits):
        bit = lax.rem(lax.div(place, 1 << b), 2)
        partners.append(place + (1 << b) * (1 - 2 * bit))

    barrier = pltpu.get_barrier_semaphore()
    for other in partners:
        pl.semaphore_signal(barrier, 1, device_id={"resp": other}, device_id_type=MESH)

    @pl.when(sec > 0)
    def _():
        pl.semaphore_signal(barrier, 1, device_id={"section": sec - 1}, device_id_type=MESH)

    @pl.when(sec < sections - 1)
    def _():
        pl.semaphore_signal(barrier, 1, device_id={"section": sec + 1}, device_id_type=MESH)

    @pl.when(sec == 0)
    def _():
        carry[...] = jnp.zeros_like(carry)

    load_p.wait()
    for g in range(kvw // HEAD):
        cols = slice(g * HEAD, (g + 1) * HEAD)
        vt_own[cols, :] = p_v[:, kvw + g * HEAD : kvw + (g + 1) * HEAD].T

    inside = (sec > 0) & (sec < sections - 1)

    @pl.when(inside)
    def _():
        pl.semaphore_wait(barrier, bits + 2)

    @pl.when(jnp.logical_not(inside))
    def _():
        pl.semaphore_wait(barrier, bits + 1)

    def exchange(b):
        if b == 0:
            sources = (p_v.at[:, 0:kvw], vt_own)
        else:
            sources = (k_all.at[0:plen, :], v_all.at[:, 0:plen])
        copies = []
        for n, (source, target) in enumerate(zip(sources, (k_in, v_in))):
            copies.append(
                pltpu.make_async_remote_copy(
                    src_ref=source,
                    dst_ref=target.at[b],
                    send_sem=x_send.at[b, n],
                    recv_sem=x_recv.at[b, n],
                    device_id={"resp": partners[b]},
                    device_id_type=MESH,
                )
            )
            copies[-1].start()
        return copies

    copies = exchange(0) if bits else None

    load_r.wait()
    load_q.wait()
    k_all[plen : plen + near, :] = r_v[:, 0:kvw]
    for g in range(kvw // HEAD):
        cols = slice(g * HEAD, (g + 1) * HEAD)
        v_all[cols, plen : plen + near] = r_v[:, kvw + g * HEAD : kvw + (g + 1) * HEAD].T

    def turn_queries(i, unused):
        both = q_v[pl.ds(pl.multiple_of(i * 16, 16), 16), :].astype(F32)
        for half in range(2):
            part = both[half * CHUNK : (half + 1) * CHUNK, :]
            for p in range(pairs):
                heads = [
                    part[:, (p * 16 + j) * HEAD : (p * 16 + j + 1) * HEAD] for j in range(16)
                ]
                q_t[2 * i + half, p * HEAD : (p + 1) * HEAD, :] = jnp.concatenate(heads, 0).T
        return unused

    lax.fori_loop(0, chunks // 2, turn_queries, 0)

    root = lax.rem(owner[0, block], group)
    if not bits:
        k_all[0:plen, :] = p_v[:, 0:kvw]
        v_all[:, 0:plen] = vt_own[...]
    for b in range(bits):
        if b:
            copies = exchange(b)
        keep = lax.div(rank, 1 << b) == lax.div(root, 1 << b)
        copies[0].wait()
        held = p_v[:, 0:kvw] if b == 0 else k_all[0:plen, :]
        k_all[0:plen, :] = jnp.where(keep, held, k_in[b])
        copies[1].wait()
        held = vt_own[...] if b == 0 else v_all[:, 0:plen]
        v_all[:, 0:plen] = jnp.where(keep, held, v_in[b])

    lane = lax.broadcasted_iota(jnp.int32, (1, HEAD), 1)
    lower = lane < HEAD // 2
    key_row = lax.broadcasted_iota(jnp.int32, (near, HEAD), 0)
    key_pos = lax.rem(key_row, TOKM)
    lane_row = lax.rem(lax.broadcasted_iota(jnp.int32, (near, HEAD), 1), CHUNK)
    factor = math.log2(math.e) / math.sqrt(HEAD)

    def forward(c):
        return pltpu.make_async_remote_copy(
            src_ref=sent.at[c],
            dst_ref=carry.at[c],
            send_sem=c_send.at[c],
            recv_sem=c_recv.at[c],
            device_id={"section": sec + 1},
            device_id_type=MESH,
        )

    def arrival(c):
        return pltpu.make_async_remote_copy(
            src_ref=sent.at[c],
            dst_ref=carry.at[c],
            send_sem=c_send.at[c],
            recv_sem=c_recv.at[c],
            device_id={"section": sec - 1},
            device_id_type=MESH,
        )

    def one_chunk(c, half):
        micro = lax.div(c * CHUNK, TOKM)
        row_pos = lane_row + lax.rem(c * CHUNK, TOKM)
        end = 0
        row_resp = jnp.zeros((near, HEAD), jnp.int32)
        key_resp = jnp.zeros((near, HEAD), jnp.int32)
        for n in range(RESPS):
            end = end + seg[micro, n]
            row_resp = row_resp + (row_pos >= end).astype(jnp.int32)
            key_resp = key_resp + (key_pos >= end).astype(jnp.int32)
        same_micro = lax.div(key_row, TOKM) == micro
        allowed = same_micro & (row_resp == key_resp) & (key_pos <= row_pos)

        @pl.when(sec > 0)
        def _():
            arrival(c).wait_recv()

        attended = []
        square = jnp.zeros((1, HEAD), F32)
        for p in range(pairs):
            part = slice(p * HEAD, (p + 1) * HEAD)
            both = slice(2 * p * HEAD, 2 * (p + 1) * HEAD)
            x = q_t[c, part, :] + carry[c, part, :].astype(F32)
            x = jnp.concatenate([jnp.where(lower, x, 0.0), jnp.where(lower, 0.0, x)], 0)
            s = jnp.dot(k_all[:, both], x.astype(BF16), preferred_element_type=F32)
            far, close = s[0:plen], jnp.where(allowed, s[plen:], -jnp.inf)
            top = jnp.maximum(
                jnp.max(far, axis=0, keepdims=True), jnp.max(close, axis=0, keepdims=True)
            )
            e = jnp.exp2((jnp.concatenate([far, close], 0) - top) * factor)
            total = jnp.sum(e, axis=0, keepdims=True)
            o = jnp.dot(v_all[both, :], e.astype(BF16), preferred_element_type=F32)
            o = jnp.where(lower, o[0:HEAD], o[HEAD:]) * (1.0 / total)
            attended.append(o)
            square = square + jnp.sum(o * o, axis=0, keepdims=True)
        square = jnp.broadcast_to(square, (8, HEAD))
        for distance in (8, 16, 32, 64):
            square = square + pltpu.roll(square, distance, 1)
        norm = lax.rsqrt(square[0:1] * (1.0 / wide) + EPS)
        for p in range(pairs):
            attended[p] = attended[p] * norm
            sent[c, p * HEAD : (p + 1) * HEAD, :] = attended[p].astype(BF16)

        @pl.when(sec < sections - 1)
        def _():
            forward(c).start()

        for p in range(pairs):
            turned = attended[p].T
            for j in range(16):
                rows16[
                    half * CHUNK : (half + 1) * CHUNK, (p * 16 + j) * HEAD : (p * 16 + j + 1) * HEAD
                ] = turned[j * CHUNK : (j + 1) * CHUNK, :]

    def store(i):
        rows = pl.ds(pl.multiple_of(i * 16, 16), 16)
        return pltpu.make_async_copy(out_v.at[rows, :], out_hbm.at[0, rows, :], out_sem.at[i])

    def two_chunks(i, unused):
        for half in range(2):
            one_chunk(2 * i + half, half)
        out_v[pl.ds(pl.multiple_of(i * 16, 16), 16), :] = rows16[...].astype(BF16)
        store(i).start()
        return unused

    lax.fori_loop(0, chunks // 2, two_chunks, 0)

    def finish(i, unused):
        store(i).wait()

        @pl.when(sec < sections - 1)
        def _():
            forward(2 * i).wait_send()
            forward(2 * i + 1).wait_send()

        return unused

    lax.fori_loop(0, chunks // 2, finish, 0)


def local(sections, bits, queries, resp_kv, prefix_kv, owner, seg_len):
    _, near, wide = queries.shape
    _, plen, kv2 = prefix_kv.shape
    kvw = kv2 // 2
    chunks = near // CHUNK
    pair_rows = kvw // 2
    steps = max(bits, 1)
    return pl.pallas_call(
        functools.partial(kernel, sections, bits),
        out_shape=jax.ShapeDtypeStruct(queries.shape, BF16),
        in_specs=[pl.BlockSpec(memory_space=pl.ANY)] * 3
        + [pl.BlockSpec(memory_space=pltpu.SMEM)] * 2,
        out_specs=pl.BlockSpec(memory_space=pl.ANY),
        scratch_shapes=[
            pltpu.VMEM((near, wide), BF16),
            pltpu.VMEM((near, kv2), BF16),
            pltpu.VMEM((plen, kv2), BF16),
            pltpu.VMEM((kvw, plen), BF16),
            pltpu.VMEM((steps, plen, kvw), BF16),
            pltpu.VMEM((steps, kvw, plen), BF16),
            pltpu.VMEM((plen + near, kvw), BF16),
            pltpu.VMEM((kvw, plen + near), BF16),
            pltpu.VMEM((chunks, pair_rows, HEAD), F32),
            pltpu.VMEM((chunks, pair_rows, HEAD), BF16),
            pltpu.VMEM((chunks, pair_rows, HEAD), BF16),
            pltpu.VMEM((16, wide), F32),
            pltpu.VMEM((near, wide), BF16),
            pltpu.SemaphoreType.DMA((3,)),
            pltpu.SemaphoreType.DMA((chunks // 2,)),
            pltpu.SemaphoreType.DMA((steps, 2)),
            pltpu.SemaphoreType.DMA((steps, 2)),
            pltpu.SemaphoreType.DMA((chunks,)),
            pltpu.SemaphoreType.DMA((chunks,)),
        ],
        compiler_params=pltpu.CompilerParams(
            collective_id=0, has_side_effects=True, vmem_limit_bytes=60 * 1024 * 1024
        ),
        cost_estimate=pl.CostEstimate(
            flops=4 * near * wide * (plen + TOKM),
            bytes_accessed=4 * near * wide + 2 * (plen + near) * kv2,
            transcendentals=near * (wide // HEAD) * (plen + TOKM),
        ),
        name="layers",
    )(queries, resp_kv, prefix_kv, owner, seg_len)


def solution(mesh):
    sections = mesh.shape["section"]
    group = mesh.shape["resp"] // PROMPTS
    return jax.shard_map(
        functools.partial(local, sections, group.bit_length() - 1),
        mesh=mesh,
        in_specs=(
            P("section", "resp", None),
            P("section", "resp", None),
            P("section", "resp", None),
            P("section", None),
            P("resp", None),
        ),
        out_specs=P("section", "resp", None),
        check_vma=False,
    )
```

time: 68.3 us -> 33.4 us (0.49)
  the two profiles are of different devices: /device:TPU:28 before, /device:TPU:30 now
where the time goes in v1:
time: 33.4 us; the launch traced here: 33.2 us
  Pallas kernels  31.3 us (94%)
  local copies, waits for them, and re-layouts  1.87 us (6%)
    pallas_call x1, Pallas kernels, local(): pl.pallas_call(functools.partial(kernel, sections, bits), out_shape=jax.S...  31.3 us
    unnamed x1, local copies, waits for them, and re-layouts  1.87 us

profile of v1, /device:TPU:30, one launch (start us, length us, event | category | flops | bytes accessed | tf_op | source)
XLA Modules:
  0.0 33.2 jit_solution(11055479087272072979)
XLA Ops:
  0.0 31.3 %layers.1 = bf16[1,64,4096]{2,1,0:T(8,128)(2,1)} custom-call(bf16[1,64,4096]{2,1,0:T(8,128)(2,1)} %q_hbm.1, bf16[1,64,1024]{2,1,0:T(8,128)(2,1)} %r_hbm.1, bf16[1,512,1024]{2,1,0:T(8,128)(2,1)} %p_hbm.1, s32[1,4]{1,0:T(1,128)} %owner.1, s32[2,4]{1,0:T(2,128)} %seg.1), custom_call_target="tpu_custom_call" | custom-call | flops 570425344 | bytes 2228224 | tf_op jit(solution)/shard_map/layers/pallas_call | solution.py:279
  31.3 1.9 %copy.7 = bf16[1,64,4096]{2,1,0:T(8,128)(2,1)} copy(bf16[1,64,4096]{2,1,0:T(8,128)(2,1)} %layers.1) | data formatting | bytes 1048576

commit v2 on v1

--- a/solution.py
+++ b/solution.py
@@ -29,7 +29,7 @@
     p_hbm,
     owner,
     seg,
-    out_hbm,
+    sent,
     q_v,
     r_v,
     p_v,
@@ -40,11 +40,8 @@
     v_all,
     q_t,
     carry,
-    sent,
-    rows16,
-    out_v,
+    bias,
     load_sem,
-    out_sem,
     x_send,
     x_recv,
     c_send,
@@ -147,6 +144,25 @@
 
     lax.fori_loop(0, chunks // 2, turn_queries, 0)
 
+    lane = lax.broadcasted_iota(jnp.int32, (1, HEAD), 1)
+    lower = lane < HEAD // 2
+    lane_row = lane & (CHUNK - 1)
+    key_row = lax.broadcasted_iota(jnp.int32, (near, HEAD), 0)
+    key_pos = key_row & (TOKM - 1)
+    for micro in range(MB):
+        key_resp = jnp.where(key_row - key_pos == micro * TOKM, 0, -1)
+        ends = []
+        for n in range(RESPS):
+            ends.append((ends[-1] if n else 0) + seg[micro, n])
+            key_resp = key_resp + jnp.where((key_pos >= ends[n]) & (key_resp >= 0), 1, 0)
+        for part in range(TOKM // CHUNK):
+            row_pos = lane_row + part * CHUNK
+            row_resp = jnp.zeros((1, HEAD), jnp.int32)
+            for end in ends:
+                row_resp = row_resp + jnp.where(row_pos >= end, 1, 0)
+            allowed = (key_resp == row_resp) & (key_pos <= row_pos)
+            bias[micro * (TOKM // CHUNK) + part] = jnp.where(allowed, 0.0, -jnp.inf)
+
     root = lax.rem(owner[0, block], group)
     if not bits:
         k_all[0:plen, :] = p_v[:, 0:kvw]
@@ -162,11 +178,6 @@
         held = vt_own[...] if b == 0 else v_all[:, 0:plen]
         v_all[:, 0:plen] = jnp.where(keep, held, v_in[b])
 
-    lane = lax.broadcasted_iota(jnp.int32, (1, HEAD), 1)
-    lower = lane < HEAD // 2
-    key_row = lax.broadcasted_iota(jnp.int32, (near, HEAD), 0)
-    key_pos = lax.rem(key_row, TOKM)
-    lane_row = lax.rem(lax.broadcasted_iota(jnp.int32, (near, HEAD), 1), CHUNK)
     factor = math.log2(math.e) / math.sqrt(HEAD)
 
     def forward(c):
@@ -189,19 +200,7 @@
             device_id_type=MESH,
         )
 
-    def one_chunk(c, half):
-        micro = lax.div(c * CHUNK, TOKM)
-        row_pos = lane_row + lax.rem(c * CHUNK, TOKM)
-        end = 0
-        row_resp = jnp.zeros((near, HEAD), jnp.int32)
-        key_resp = jnp.zeros((near, HEAD), jnp.int32)
-        for n in range(RESPS):
-            end = end + seg[micro, n]
-            row_resp = row_resp + (row_pos >= end).astype(jnp.int32)
-            key_resp = key_resp + (key_pos >= end).astype(jnp.int32)
-        same_micro = lax.div(key_row, TOKM) == micro
-        allowed = same_micro & (row_resp == key_resp) & (key_pos <= row_pos)
-
+    def one_chunk(c):
         @pl.when(sec > 0)
         def _():
             arrival(c).wait_recv()
@@ -214,7 +213,7 @@
             x = q_t[c, part, :] + carry[c, part, :].astype(F32)
             x = jnp.concatenate([jnp.where(lower, x, 0.0), jnp.where(lower, 0.0, x)], 0)
             s = jnp.dot(k_all[:, both], x.astype(BF16), preferred_element_type=F32)
-            far, close = s[0:plen], jnp.where(allowed, s[plen:], -jnp.inf)
+            far, close = s[0:plen], s[plen:] + bias[c]
             top = jnp.maximum(
                 jnp.max(far, axis=0, keepdims=True), jnp.max(close, axis=0, keepdims=True)
             )
@@ -229,44 +228,38 @@
             square = square + pltpu.roll(square, distance, 1)
         norm = lax.rsqrt(square[0:1] * (1.0 / wide) + EPS)
         for p in range(pairs):
-            attended[p] = attended[p] * norm
-            sent[c, p * HEAD : (p + 1) * HEAD, :] = attended[p].astype(BF16)
+            sent[c, p * HEAD : (p + 1) * HEAD, :] = (attended[p] * norm).astype(BF16)
 
         @pl.when(sec < sections - 1)
         def _():
             forward(c).start()
 
+    def step(c, unused):
+        one_chunk(c)
+        return unused
+
+    lax.fori_loop(0, chunks, step, 0)
+
+    @pl.when(sec < sections - 1)
+    def _():
+        def finish(c, unused):
+            forward(c).wait_send()
+            return unused
+
+        lax.fori_loop(0, chunks, finish, 0)
+
+
+def turn_kernel(pairs, turned, out):
+    for i in range(turned.shape[0] // 2):
         for p in range(pairs):
-            turned = attended[p].T
+            part = slice(p * HEAD, (p + 1) * HEAD)
+            first = turned[2 * i, part, :].astype(F32).T
+            second = turned[2 * i + 1, part, :].astype(F32).T
             for j in range(16):
-                rows16[
-                    half * CHUNK : (half + 1) * CHUNK, (p * 16 + j) * HEAD : (p * 16 + j + 1) * HEAD
-                ] = turned[j * CHUNK : (j + 1) * CHUNK, :]
-
-    def store(i):
-        rows = pl.ds(pl.multiple_of(i * 16, 16), 16)
-        return pltpu.make_async_copy(out_v.at[rows, :], out_hbm.at[0, rows, :], out_sem.at[i])
-
-    def two_chunks(i, unused):
-        for half in range(2):
-            one_chunk(2 * i + half, half)
-        out_v[pl.ds(pl.multiple_of(i * 16, 16), 16), :] = rows16[...].astype(BF16)
-        store(i).start()
-        return unused
-
-    lax.fori_loop(0, chunks // 2, two_chunks, 0)
-
-    def finish(i, unused):
-        store(i).wait()
-
-        @pl.when(sec < sections - 1)
-        def _():
-            forward(2 * i).wait_send()
-            forward(2 * i + 1).wait_send()
-
-        return unused
-
-    lax.fori_loop(0, chunks // 2, finish, 0)
+                rows = slice(j * CHUNK, (j + 1) * CHUNK)
+                both = jnp.concatenate([first[rows], second[rows]], 0)
+                column = (p * 16 + j) * HEAD
+                out[0, 16 * i : 16 * (i + 1), column : column + HEAD] = both.astype(BF16)
 
 
 def local(sections, bits, queries, resp_kv, prefix_kv, owner, seg_len):
@@ -276,12 +269,12 @@
     chunks = near // CHUNK
     pair_rows = kvw // 2
     steps = max(bits, 1)
-    return pl.pallas_call(
+    turned = pl.pallas_call(
         functools.partial(kernel, sections, bits),
-        out_shape=jax.ShapeDtypeStruct(queries.shape, BF16),
+        out_shape=jax.ShapeDtypeStruct((chunks, pair_rows, HEAD), BF16),
         in_specs=[pl.BlockSpec(memory_space=pl.ANY)] * 3
         + [pl.BlockSpec(memory_space=pltpu.SMEM)] * 2,
-        out_specs=pl.BlockSpec(memory_space=pl.ANY),
+        out_specs=pl.BlockSpec(memory_space=pltpu.VMEM),
         scratch_shapes=[
             pltpu.VMEM((near, wide), BF16),
             pltpu.VMEM((near, kv2), BF16),
@@ -293,11 +286,8 @@
             pltpu.VMEM((kvw, plen + near), BF16),
             pltpu.VMEM((chunks, pair_rows, HEAD), F32),
             pltpu.VMEM((chunks, pair_rows, HEAD), BF16),
-            pltpu.VMEM((chunks, pair_rows, HEAD), BF16),
-            pltpu.VMEM((16, wide), F32),
-            pltpu.VMEM((near, wide), BF16),
+            pltpu.VMEM((chunks, near, HEAD), F32),
             pltpu.SemaphoreType.DMA((3,)),
-            pltpu.SemaphoreType.DMA((chunks // 2,)),
             pltpu.SemaphoreType.DMA((steps, 2)),
             pltpu.SemaphoreType.DMA((steps, 2)),
             pltpu.SemaphoreType.DMA((chunks,)),
@@ -313,6 +303,15 @@
         ),
         name="layers",
     )(queries, resp_kv, prefix_kv, owner, seg_len)
+    parts = 2
+    return pl.pallas_call(
+        functools.partial(turn_kernel, kvw // (2 * HEAD)),
+        grid=(parts,),
+        out_shape=jax.ShapeDtypeStruct(queries.shape, BF16),
+        in_specs=[pl.BlockSpec((chunks // parts, pair_rows, HEAD), lambda i: (i, 0, 0))],
+        out_specs=pl.BlockSpec((1, near // parts, wide), lambda i: (0, i, 0)),
+        name="turn",
+    )(turned)
 
 
 def solution(mesh):

time: 33.4 us -> 32.6 us (0.976)
  local copies, waits for them, and re-layouts: 1.87 us -> 0 us
  Pallas kernels: 31.3 us -> 32.4 us
    pallas_call x0 -> x1, Pallas kernels: none -> 1.96 us  [local(): pl.pallas_call(functools.partial(turn_kernel, kvw // (2 * HEAD)), grid=(p...]
    unnamed x1 -> x0, local copies, waits for them, and re-layouts: 1.87 us -> none
    pallas_call x1, Pallas kernels: 31.3 us -> 30.5 us  [local(): pl.pallas_call(functools.partial(kernel, sections, bits), out_shape=jax.S...]
where the time goes in v2:
time: 32.6 us; the launch traced here: 32.4 us
  Pallas kernels  32.4 us (99%)
    pallas_call x1, Pallas kernels, local(): pl.pallas_call(functools.partial(kernel, sections, bits), out_shape=jax.S...  30.5 us
    pallas_call x1, Pallas kernels, local(): pl.pallas_call(functools.partial(turn_kernel, kvw // (2 * HEAD)), grid=(p...  1.96 us

profile of v2, /device:TPU:30, one launch (start us, length us, event | category | flops | bytes accessed | tf_op | source)
XLA Modules:
  0.0 32.4 jit_solution(2956499077879421619)
XLA Ops:
  0.0 30.5 %layers.1.turned = bf16[8,256,128]{2,1,0:T(8,128)(2,1)} custom-call(bf16[1,64,4096]{2,1,0:T(8,128)(2,1)} %q_hbm.1, bf16[1,64,1024]{2,1,0:T(8,128)(2,1)} %r_hbm.1, bf16[1,512,1024]{2,1,0:T(8,128)(2,1)} %p_hbm.1, s32[1,4]{1,0:T(1,128)} %owner.1, s32[2,4]{1,0:T(2,128)} %seg.1), custom_call_target="tpu_custom_call" | custom-call | flops 570425344 | bytes 2228224 | tf_op jit(solution)/shard_map/layers/pallas_call | solution.py:272
  30.5 2.0 %turn.1 = bf16[1,64,4096]{2,1,0:T(8,128)(2,1)} custom-call(bf16[8,256,128]{2,1,0:T(8,128)(2,1)} %layers.1.turned), custom_call_target="tpu_custom_call" | custom-call | tf_op jit(solution)/shard_map/turn/pallas_call | solution.py:307

commit v3 on v2

--- a/solution.py
+++ b/solution.py
@@ -29,7 +29,7 @@
     p_hbm,
     owner,
     seg,
-    sent,
+    done_hbm,
     q_v,
     r_v,
     p_v,
@@ -40,8 +40,10 @@
     v_all,
     q_t,
     carry,
+    sent,
     bias,
     load_sem,
+    done_sem,
     x_send,
     x_recv,
     c_send,
@@ -87,10 +89,13 @@
     def _():
         carry[...] = jnp.zeros_like(carry)
 
+    def turn_values(p):
+        for g in (2 * p, 2 * p + 1):
+            cols = slice(g * HEAD, (g + 1) * HEAD)
+            vt_own[cols, :] = p_v[:, kvw + g * HEAD : kvw + (g + 1) * HEAD].T
+
     load_p.wait()
-    for g in range(kvw // HEAD):
-        cols = slice(g * HEAD, (g + 1) * HEAD)
-        vt_own[cols, :] = p_v[:, kvw + g * HEAD : kvw + (g + 1) * HEAD].T
+    turn_values(0)
 
     inside = (sec > 0) & (sec < sections - 1)
 
@@ -102,19 +107,21 @@
     def _():
         pl.semaphore_wait(barrier, bits + 1)
 
-    def exchange(b):
+    def exchange(b, p):
+        both = slice(2 * p * HEAD, 2 * (p + 1) * HEAD)
         if b == 0:
-            sources = (p_v.at[:, 0:kvw], vt_own)
+            sources = (p_v.at[:, both], vt_own.at[both, :])
         else:
-            sources = (k_all.at[0:plen, :], v_all.at[:, 0:plen])
+            sources = (k_all.at[0:plen, both], v_all.at[both, 0:plen])
+        targets = (k_in.at[b, :, both], v_in.at[b, both, :])
         copies = []
-        for n, (source, target) in enumerate(zip(sources, (k_in, v_in))):
+        for n, (source, target) in enumerate(zip(sources, targets)):
             copies.append(
                 pltpu.make_async_remote_copy(
                     src_ref=source,
-                    dst_ref=target.at[b],
-                    send_sem=x_send.at[b, n],
-                    recv_sem=x_recv.at[b, n],
+                    dst_ref=target,
+                    send_sem=x_send.at[b, p, n],
+                    recv_sem=x_recv.at[b, p, n],
                     device_id={"resp": partners[b]},
                     device_id_type=MESH,
                 )
@@ -122,7 +129,12 @@
             copies[-1].start()
         return copies
 
-    copies = exchange(0) if bits else None
+    first = []
+    for p in range(pairs):
+        if p:
+            turn_values(p)
+        if bits:
+            first.append(exchange(0, p))
 
     load_r.wait()
     load_q.wait()
@@ -164,19 +176,24 @@
             bias[micro * (TOKM // CHUNK) + part] = jnp.where(allowed, 0.0, -jnp.inf)
 
     root = lax.rem(owner[0, block], group)
-    if not bits:
-        k_all[0:plen, :] = p_v[:, 0:kvw]
-        v_all[:, 0:plen] = vt_own[...]
-    for b in range(bits):
-        if b:
-            copies = exchange(b)
+
+    def settle(b, p, copies):
+        both = slice(2 * p * HEAD, 2 * (p + 1) * HEAD)
         keep = lax.div(rank, 1 << b) == lax.div(root, 1 << b)
         copies[0].wait()
-        held = p_v[:, 0:kvw] if b == 0 else k_all[0:plen, :]
-        k_all[0:plen, :] = jnp.where(keep, held, k_in[b])
+        held = p_v[:, both] if b == 0 else k_all[0:plen, both]
+        k_all[0:plen, both] = jnp.where(keep, held, k_in[b, :, both])
         copies[1].wait()
-        held = vt_own[...] if b == 0 else v_all[:, 0:plen]
-        v_all[:, 0:plen] = jnp.where(keep, held, v_in[b])
+        held = vt_own[both, :] if b == 0 else v_all[both, 0:plen]
+        v_all[both, 0:plen] = jnp.where(keep, held, v_in[b, both, :])
+
+    def prefix_ready(p):
+        both = slice(2 * p * HEAD, 2 * (p + 1) * HEAD)
+        if not bits:
+            k_all[0:plen, both] = p_v[:, both]
+            v_all[both, 0:plen] = vt_own[both, :]
+        for b in range(bits):
+            settle(b, p, first[p] if b == 0 else exchange(b, p))
 
     factor = math.log2(math.e) / math.sqrt(HEAD)
 
@@ -200,7 +217,10 @@
             device_id_type=MESH,
         )
 
-    def one_chunk(c):
+    def done(c):
+        return pltpu.make_async_copy(sent.at[c], done_hbm.at[c], done_sem.at[c])
+
+    def one_chunk(c, ready=None):
         @pl.when(sec > 0)
         def _():
             arrival(c).wait_recv()
@@ -210,6 +230,8 @@
         for p in range(pairs):
             part = slice(p * HEAD, (p + 1) * HEAD)
             both = slice(2 * p * HEAD, 2 * (p + 1) * HEAD)
+            if ready is not None:
+                ready(p)
             x = q_t[c, part, :] + carry[c, part, :].astype(F32)
             x = jnp.concatenate([jnp.where(lower, x, 0.0), jnp.where(lower, 0.0, x)], 0)
             s = jnp.dot(k_all[:, both], x.astype(BF16), preferred_element_type=F32)
@@ -219,8 +241,9 @@
             )
             e = jnp.exp2((jnp.concatenate([far, close], 0) - top) * factor)
             total = jnp.sum(e, axis=0, keepdims=True)
+            e = e * (1.0 / total)
             o = jnp.dot(v_all[both, :], e.astype(BF16), preferred_element_type=F32)
-            o = jnp.where(lower, o[0:HEAD], o[HEAD:]) * (1.0 / total)
+            o = jnp.where(lower, o[0:HEAD], o[HEAD:])
             attended.append(o)
             square = square + jnp.sum(o * o, axis=0, keepdims=True)
         square = jnp.broadcast_to(square, (8, HEAD))
@@ -234,23 +257,36 @@
         def _():
             forward(c).start()
 
+        done(c).start()
+
     def step(c, unused):
         one_chunk(c)
         return unused
 
-    lax.fori_loop(0, chunks, step, 0)
-
-    @pl.when(sec < sections - 1)
-    def _():
-        def finish(c, unused):
+    one_chunk(0, prefix_ready)
+    lax.fori_loop(1, chunks, step, 0)
+
+    def finish(c, unused):
+        done(c).wait()
+
+        @pl.when(sec < sections - 1)
+        def _():
             forward(c).wait_send()
-            return unused
-
-        lax.fori_loop(0, chunks, finish, 0)
-
-
-def turn_kernel(pairs, turned, out):
-    for i in range(turned.shape[0] // 2):
+
+        return unused
+
+    lax.fori_loop(0, chunks, finish, 0)
+
+
+def turn_kernel(pairs, turned_hbm, out_hbm, turned, out, in_sem, out_sem):
+    parts = turned.shape[0] // 2
+    loads, stores = [], []
+    for i in range(parts):
+        chunk = slice(2 * i, 2 * i + 2)
+        loads.append(pltpu.make_async_copy(turned_hbm.at[chunk], turned.at[chunk], in_sem.at[i]))
+        loads[-1].start()
+    for i in range(parts):
+        loads[i].wait()
         for p in range(pairs):
             part = slice(p * HEAD, (p + 1) * HEAD)
             first = turned[2 * i, part, :].astype(F32).T
@@ -259,7 +295,12 @@
                 rows = slice(j * CHUNK, (j + 1) * CHUNK)
                 both = jnp.concatenate([first[rows], second[rows]], 0)
                 column = (p * 16 + j) * HEAD
-                out[0, 16 * i : 16 * (i + 1), column : column + HEAD] = both.astype(BF16)
+                out[16 * i : 16 * (i + 1), column : column + HEAD] = both.astype(BF16)
+        rows = slice(16 * i, 16 * (i + 1))
+        stores.append(pltpu.make_async_copy(out.at[rows], out_hbm.at[0, rows], out_sem.at[i]))
+        stores[-1].start()
+    for copy in stores:
+        copy.wait()
 
 
 def local(sections, bits, queries, resp_kv, prefix_kv, owner, seg_len):
@@ -274,7 +315,7 @@
         out_shape=jax.ShapeDtypeStruct((chunks, pair_rows, HEAD), BF16),
         in_specs=[pl.BlockSpec(memory_space=pl.ANY)] * 3
         + [pl.BlockSpec(memory_space=pltpu.SMEM)] * 2,
-        out_specs=pl.BlockSpec(memory_space=pltpu.VMEM),
+        out_specs=pl.BlockSpec(memory_space=pl.ANY),
         scratch_shapes=[
             pltpu.VMEM((near, wide), BF16),
             pltpu.VMEM((near, kv2), BF16),
@@ -286,10 +327,12 @@
             pltpu.VMEM((kvw, plen + near), BF16),
             pltpu.VMEM((chunks, pair_rows, HEAD), F32),
             pltpu.VMEM((chunks, pair_rows, HEAD), BF16),
+            pltpu.VMEM((chunks, pair_rows, HEAD), BF16),
             pltpu.VMEM((chunks, near, HEAD), F32),
             pltpu.SemaphoreType.DMA((3,)),
-            pltpu.SemaphoreType.DMA((steps, 2)),
-            pltpu.SemaphoreType.DMA((steps, 2)),
+            pltpu.SemaphoreType.DMA((chunks,)),
+            pltpu.SemaphoreType.DMA((steps, 2, 2)),
+            pltpu.SemaphoreType.DMA((steps, 2, 2)),
             pltpu.SemaphoreType.DMA((chunks,)),
             pltpu.SemaphoreType.DMA((chunks,)),
         ],
@@ -303,13 +346,18 @@
         ),
         name="layers",
     )(queries, resp_kv, prefix_kv, owner, seg_len)
-    parts = 2
     return pl.pallas_call(
         functools.partial(turn_kernel, kvw // (2 * HEAD)),
-        grid=(parts,),
         out_shape=jax.ShapeDtypeStruct(queries.shape, BF16),
-        in_specs=[pl.BlockSpec((chunks // parts, pair_rows, HEAD), lambda i: (i, 0, 0))],
-        out_specs=pl.BlockSpec((1, near // parts, wide), lambda i: (0, i, 0)),
+        in_specs=[pl.BlockSpec(memory_space=pl.ANY)],
+        out_specs=pl.BlockSpec(memory_space=pl.ANY),
+        scratch_shapes=[
+            pltpu.VMEM((chunks, pair_rows, HEAD), BF16),
+            pltpu.VMEM((near, wide), BF16),
+            pltpu.SemaphoreType.DMA((chunks // 2,)),
+            pltpu.SemaphoreType.DMA((chunks // 2,)),
+        ],
+        compiler_params=pltpu.CompilerParams(vmem_limit_bytes=60 * 1024 * 1024),
         name="turn",
     )(turned)
 

time: 32.6 us -> 33.8 us (1.037)
  Pallas kernels: 32.4 us -> 33.6 us
    pallas_call x1, Pallas kernels: 30.5 us -> 31.6 us  [local(): pl.pallas_call(functools.partial(kernel, sections, bits), out_shape=jax.S...]
where the time goes in v3:
time: 33.8 us; the launch traced here: 33.6 us
  Pallas kernels  33.6 us (99%)
    pallas_call x1, Pallas kernels, local(): pl.pallas_call(functools.partial(kernel, sections, bits), out_shape=jax.S...  31.6 us
    pallas_call x1, Pallas kernels, local(): pl.pallas_call(functools.partial(turn_kernel, kvw // (2 * HEAD)), out_sha...  2.06 us

profile of v3, /device:TPU:30, one launch (start us, length us, event | category | flops | bytes accessed | tf_op | source)
XLA Modules:
  0.0 33.6 jit_solution(9550183900314635272)
XLA Ops:
  0.0 31.6 %layers.1.turned_hbm = bf16[8,256,128]{2,1,0:T(8,128)(2,1)} custom-call(bf16[1,64,4096]{2,1,0:T(8,128)(2,1)} %q_hbm.1, bf16[1,64,1024]{2,1,0:T(8,128)(2,1)} %r_hbm.1, bf16[1,512,1024]{2,1,0:T(8,128)(2,1)} %p_hbm.1, s32[1,4]{1,0:T(1,128)} %owner.1, s32[2,4]{1,0:T(2,128)} %seg.1), custom_call_target="tpu_custom_call" | custom-call | flops 570425344 | bytes 2228224 | tf_op jit(solution)/shard_map/layers/pallas_call | solution.py:313
  31.6 2.1 %turn.1 = bf16[1,64,4096]{2,1,0:T(8,128)(2,1)} custom-call(bf16[8,256,128]{2,1,0:T(8,128)(2,1)} %layers.1.turned_hbm), custom_call_target="tpu_custom_call" | custom-call | tf_op jit(solution)/shard_map/turn/pallas_call | solution.py:349

commit v4 on v3

--- a/solution.py
+++ b/solution.py
@@ -241,9 +241,8 @@
             )
             e = jnp.exp2((jnp.concatenate([far, close], 0) - top) * factor)
             total = jnp.sum(e, axis=0, keepdims=True)
-            e = e * (1.0 / total)
             o = jnp.dot(v_all[both, :], e.astype(BF16), preferred_element_type=F32)
-            o = jnp.where(lower, o[0:HEAD], o[HEAD:])
+            o = jnp.where(lower, o[0:HEAD], o[HEAD:]) * (1.0 / total)
             attended.append(o)
             square = square + jnp.sum(o * o, axis=0, keepdims=True)
         square = jnp.broadcast_to(square, (8, HEAD))

time: 33.8 us -> 33.6 us (level)
  no operation moved by 1% of the time
where the time goes in v4:
time: 33.6 us; the launch traced here: 33.4 us
  Pallas kernels  33.4 us (99%)
    pallas_call x1, Pallas kernels, local(): pl.pallas_call(functools.partial(kernel, sections, bits), out_shape=jax.S...  31.4 us
    pallas_call x1, Pallas kernels, local(): pl.pallas_call(functools.partial(turn_kernel, kvw // (2 * HEAD)), out_sha...  2.06 us

profile of v4, /device:TPU:30, one launch (start us, length us, event | category | flops | bytes accessed | tf_op | source)
XLA Modules:
  0.0 33.4 jit_solution(3683644162465245593)
XLA Ops:
  0.0 31.4 %layers.1.turned_hbm = bf16[8,256,128]{2,1,0:T(8,128)(2,1)} custom-call(bf16[1,64,4096]{2,1,0:T(8,128)(2,1)} %q_hbm.1, bf16[1,64,1024]{2,1,0:T(8,128)(2,1)} %r_hbm.1, bf16[1,512,1024]{2,1,0:T(8,128)(2,1)} %p_hbm.1, s32[1,4]{1,0:T(1,128)} %owner.1, s32[2,4]{1,0:T(2,128)} %seg.1), custom_call_target="tpu_custom_call" | custom-call | flops 570425344 | bytes 2228224 | tf_op jit(solution)/shard_map/layers/pallas_call | solution.py:312
  31.4 2.1 %turn.1 = bf16[1,64,4096]{2,1,0:T(8,128)(2,1)} custom-call(bf16[8,256,128]{2,1,0:T(8,128)(2,1)} %layers.1.turned_hbm), custom_call_target="tpu_custom_call" | custom-call | tf_op jit(solution)/shard_map/turn/pallas_call | solution.py:348

commit v5 on v2

--- a/solution.py
+++ b/solution.py
@@ -33,11 +33,8 @@
     q_v,
     r_v,
     p_v,
-    vt_own,
-    k_in,
-    v_in,
-    k_all,
-    v_all,
+    kv_in,
+    kv_all,
     q_t,
     carry,
     bias,
@@ -88,10 +85,6 @@
         carry[...] = jnp.zeros_like(carry)
 
     load_p.wait()
-    for g in range(kvw // HEAD):
-        cols = slice(g * HEAD, (g + 1) * HEAD)
-        vt_own[cols, :] = p_v[:, kvw + g * HEAD : kvw + (g + 1) * HEAD].T
-
     inside = (sec > 0) & (sec < sections - 1)
 
     @pl.when(inside)
@@ -103,16 +96,13 @@
         pl.semaphore_wait(barrier, bits + 1)
 
     def exchange(b):
-        if b == 0:
-            sources = (p_v.at[:, 0:kvw], vt_own)
-        else:
-            sources = (k_all.at[0:plen, :], v_all.at[:, 0:plen])
         copies = []
-        for n, (source, target) in enumerate(zip(sources, (k_in, v_in))):
+        for n in range(2):
+            cols = slice(n * kvw, (n + 1) * kvw)
             copies.append(
                 pltpu.make_async_remote_copy(
-                    src_ref=source,
-                    dst_ref=target.at[b],
+                    src_ref=p_v.at[:, cols] if b == 0 else kv_all.at[0:plen, cols],
+                    dst_ref=kv_in.at[b, :, cols],
                     send_sem=x_send.at[b, n],
                     recv_sem=x_recv.at[b, n],
                     device_id={"resp": partners[b]},
@@ -126,10 +116,7 @@
 
     load_r.wait()
     load_q.wait()
-    k_all[plen : plen + near, :] = r_v[:, 0:kvw]
-    for g in range(kvw // HEAD):
-        cols = slice(g * HEAD, (g + 1) * HEAD)
-        v_all[cols, plen : plen + near] = r_v[:, kvw + g * HEAD : kvw + (g + 1) * HEAD].T
+    kv_all[plen : plen + near, :] = r_v[...]
 
     def turn_queries(i, unused):
         both = q_v[pl.ds(pl.multiple_of(i * 16, 16), 16), :].astype(F32)
@@ -139,15 +126,13 @@
                 heads = [
                     part[:, (p * 16 + j) * HEAD : (p * 16 + j + 1) * HEAD] for j in range(16)
                 ]
-                q_t[2 * i + half, p * HEAD : (p + 1) * HEAD, :] = jnp.concatenate(heads, 0).T
+                q_t[2 * i + half, p * HEAD : (p + 1) * HEAD, :] = jnp.concatenate(heads, 0)
         return unused
 
     lax.fori_loop(0, chunks // 2, turn_queries, 0)
 
-    lane = lax.broadcasted_iota(jnp.int32, (1, HEAD), 1)
-    lower = lane < HEAD // 2
-    lane_row = lane & (CHUNK - 1)
-    key_row = lax.broadcasted_iota(jnp.int32, (near, HEAD), 0)
+    row = lax.broadcasted_iota(jnp.int32, (CHUNK, near), 0)
+    key_row = lax.broadcasted_iota(jnp.int32, (CHUNK, near), 1)
     key_pos = key_row & (TOKM - 1)
     for micro in range(MB):
         key_resp = jnp.where(key_row - key_pos == micro * TOKM, 0, -1)
@@ -156,8 +141,8 @@
             ends.append((ends[-1] if n else 0) + seg[micro, n])
             key_resp = key_resp + jnp.where((key_pos >= ends[n]) & (key_resp >= 0), 1, 0)
         for part in range(TOKM // CHUNK):
-            row_pos = lane_row + part * CHUNK
-            row_resp = jnp.zeros((1, HEAD), jnp.int32)
+            row_pos = row + part * CHUNK
+            row_resp = jnp.zeros((CHUNK, near), jnp.int32)
             for end in ends:
                 row_resp = row_resp + jnp.where(row_pos >= end, 1, 0)
             allowed = (key_resp == row_resp) & (key_pos <= row_pos)
@@ -165,18 +150,16 @@
 
     root = lax.rem(owner[0, block], group)
     if not bits:
-        k_all[0:plen, :] = p_v[:, 0:kvw]
-        v_all[:, 0:plen] = vt_own[...]
+        kv_all[0:plen, :] = p_v[...]
     for b in range(bits):
         if b:
             copies = exchange(b)
         keep = lax.div(rank, 1 << b) == lax.div(root, 1 << b)
-        copies[0].wait()
-        held = p_v[:, 0:kvw] if b == 0 else k_all[0:plen, :]
-        k_all[0:plen, :] = jnp.where(keep, held, k_in[b])
-        copies[1].wait()
-        held = vt_own[...] if b == 0 else v_all[:, 0:plen]
-        v_all[:, 0:plen] = jnp.where(keep, held, v_in[b])
+        for n in range(2):
+            cols = slice(n * kvw, (n + 1) * kvw)
+            copies[n].wait()
+            held = p_v[:, cols] if b == 0 else kv_all[0:plen, cols]
+            kv_all[0:plen, cols] = jnp.where(keep, held, kv_in[b, :, cols])
 
     factor = math.log2(math.e) / math.sqrt(HEAD)
 
@@ -206,27 +189,41 @@
             arrival(c).wait_recv()
 
         attended = []
-        square = jnp.zeros((1, HEAD), F32)
+        square = jnp.zeros((CHUNK, HEAD), F32)
+        masked = jnp.concatenate([bias[c]] * 16, 0)
+        empty = jnp.zeros((HEAD // 2, HEAD), F32)
+        middle = HEAD // 2
         for p in range(pairs):
             part = slice(p * HEAD, (p + 1) * HEAD)
-            both = slice(2 * p * HEAD, 2 * (p + 1) * HEAD)
+            keys = slice(2 * p * HEAD, 2 * (p + 1) * HEAD)
+            values = slice(kvw + 2 * p * HEAD, kvw + 2 * (p + 1) * HEAD)
             x = q_t[c, part, :] + carry[c, part, :].astype(F32)
-            x = jnp.concatenate([jnp.where(lower, x, 0.0), jnp.where(lower, 0.0, x)], 0)
-            s = jnp.dot(k_all[:, both], x.astype(BF16), preferred_element_type=F32)
-            far, close = s[0:plen], s[plen:] + bias[c]
+            x = jnp.concatenate(
+                [
+                    jnp.concatenate([x[0:middle], empty], 1),
+                    jnp.concatenate([empty, x[middle:]], 1),
+                ],
+                0,
+            ).astype(BF16)
+            over = (((1,), (1,)), ((), ()))
+            far = lax.dot_general(x, kv_all[0:plen, keys], over, preferred_element_type=F32)
+            close = lax.dot_general(x, kv_all[plen:, keys], over, preferred_element_type=F32)
+            close = close + masked
             top = jnp.maximum(
-                jnp.max(far, axis=0, keepdims=True), jnp.max(close, axis=0, keepdims=True)
+                jnp.max(far, axis=1, keepdims=True), jnp.max(close, axis=1, keepdims=True)
             )
-            e = jnp.exp2((jnp.concatenate([far, close], 0) - top) * factor)
-            total = jnp.sum(e, axis=0, keepdims=True)
-            o = jnp.dot(v_all[both, :], e.astype(BF16), preferred_element_type=F32)
-            o = jnp.where(lower, o[0:HEAD], o[HEAD:]) * (1.0 / total)
+            far = jnp.exp2((far - top) * factor)
+            close = jnp.exp2((close - top) * factor)
+            total = jnp.sum(far, axis=1, keepdims=True) + jnp.sum(close, axis=1, keepdims=True)
+            o = jnp.dot(far.astype(BF16), kv_all[0:plen, values], preferred_element_type=F32)
+            o = o + jnp.dot(close.astype(BF16), kv_all[plen:, values], preferred_element_type=F32)
+            o = jnp.concatenate([o[0:middle, 0:HEAD], o[middle:, HEAD:]], 0) * (1.0 / total)
             attended.append(o)
-            square = square + jnp.sum(o * o, axis=0, keepdims=True)
-        square = jnp.broadcast_to(square, (8, HEAD))
-        for distance in (8, 16, 32, 64):
-            square = square + pltpu.roll(square, distance, 1)
-        norm = lax.rsqrt(square[0:1] * (1.0 / wide) + EPS)
+            for j in range(16):
+                piece = o[j * CHUNK : (j + 1) * CHUNK]
+                square = square + piece * piece
+        norm = lax.rsqrt(jnp.sum(square, axis=1, keepdims=True) * (1.0 / wide) + EPS)
+        norm = jnp.concatenate([jnp.broadcast_to(norm, (CHUNK, HEAD))] * 16, 0)
         for p in range(pairs):
             sent[c, p * HEAD : (p + 1) * HEAD, :] = (attended[p] * norm).astype(BF16)
 
@@ -253,8 +250,8 @@
     for i in range(turned.shape[0] // 2):
         for p in range(pairs):
             part = slice(p * HEAD, (p + 1) * HEAD)
-            first = turned[2 * i, part, :].astype(F32).T
-            second = turned[2 * i + 1, part, :].astype(F32).T
+            first = turned[2 * i, part, :].astype(F32)
+            second = turned[2 * i + 1, part, :].astype(F32)
             for j in range(16):
                 rows = slice(j * CHUNK, (j + 1) * CHUNK)
                 both = jnp.concatenate([first[rows], second[rows]], 0)
@@ -279,14 +276,11 @@
             pltpu.VMEM((near, wide), BF16),
             pltpu.VMEM((near, kv2), BF16),
             pltpu.VMEM((plen, kv2), BF16),
-            pltpu.VMEM((kvw, plen), BF16),
-            pltpu.VMEM((steps, plen, kvw), BF16),
-            pltpu.VMEM((steps, kvw, plen), BF16),
-            pltpu.VMEM((plen + near, kvw), BF16),
-            pltpu.VMEM((kvw, plen + near), BF16),
+            pltpu.VMEM((steps, plen, kv2), BF16),
+            pltpu.VMEM((plen + near, kv2), BF16),
             pltpu.VMEM((chunks, pair_rows, HEAD), F32),
             pltpu.VMEM((chunks, pair_rows, HEAD), BF16),
-            pltpu.VMEM((chunks, near, HEAD), F32),
+            pltpu.VMEM((chunks, CHUNK, near), F32),
             pltpu.SemaphoreType.DMA((3,)),
             pltpu.SemaphoreType.DMA((steps, 2)),
             pltpu.SemaphoreType.DMA((steps, 2)),

time: 32.6 us -> 31.9 us (0.979)
  Pallas kernels: 32.4 us -> 31.7 us
    pallas_call x1, Pallas kernels: 30.5 us -> 29.9 us  [local(): pl.pallas_call(functools.partial(kernel, sections, bits), out_shape=jax.S...]
where the time goes in v5:
time: 31.9 us; the launch traced here: 31.7 us
  Pallas kernels  31.7 us (99%)
    pallas_call x1, Pallas kernels, local(): pl.pallas_call(functools.partial(kernel, sections, bits), out_shape=jax.S...  29.9 us
    pallas_call x1, Pallas kernels, local(): pl.pallas_call(functools.partial(turn_kernel, kvw // (2 * HEAD)), grid=(p...  1.79 us

profile of v5, /device:TPU:30, one launch (start us, length us, event | category | flops | bytes accessed | tf_op | source)
XLA Modules:
  0.0 31.7 jit_solution(11527502390789454321)
XLA Ops:
  0.0 29.9 %layers.1.turned = bf16[8,256,128]{2,1,0:T(8,128)(2,1)} custom-call(bf16[1,64,4096]{2,1,0:T(8,128)(2,1)} %q_hbm.1, bf16[1,64,1024]{2,1,0:T(8,128)(2,1)} %r_hbm.1, bf16[1,512,1024]{2,1,0:T(8,128)(2,1)} %p_hbm.1, s32[1,4]{1,0:T(1,128)} %owner.1, s32[2,4]{1,0:T(2,128)} %seg.1), custom_call_target="tpu_custom_call" | custom-call | flops 570425344 | bytes 2228224 | tf_op jit(solution)/shard_map/layers/pallas_call | solution.py:269
  29.9 1.8 %turn.1 = bf16[1,64,4096]{2,1,0:T(8,128)(2,1)} custom-call(bf16[8,256,128]{2,1,0:T(8,128)(2,1)} %layers.1.turned), custom_call_target="tpu_custom_call" | custom-call | tf_op jit(solution)/shard_map/turn/pallas_call | solution.py:301
